TPU v7x, 256 devices: a whole 4x4x8 slice. The times are simulated.
256 devices in a mesh: occ: 64 (over x_hi, z, y), aux: 4 (over x_lo, core).
Axes of the slice: x: 4 (x_hi: 2, x_lo: 2; x = x_hi * 2 + x_lo), y: 4, z: 8, core: 2. Of those that a mesh axis runs over, the one named last changes fastest.
Arguments:
- b_tensor: bfloat16 [24000, 256, 128], P('aux', 'occ'), may hold values from -1.25 to 1.25
- occ_energy: float32 [256], replicated, may hold values from -1.5 to -0.3
- vir_energy: float32 [128], replicated, may hold values from 0.3 to 3
- occ_count: int32 [64], replicated, may hold values from 1 to 4, 192 in all
Outputs:
- gamma: bfloat16 [24000, 256, 128], P('aux', 'occ')
Inputs may be any that keep to these rules, and one draw needn't show every extreme that they name: `occ_count`: each block has at least one live orbital; some block has all 4 live.
All inputs are finite; a program needn't handle non-finite values.
Results may differ from a plain program's by a relative error of at most 0.0048.
Values may be sent and summed in bfloat16 or wider, within the bound.
A program may use at most 128 MiB of HBM per device.

v0:
```python
import jax
import jax.numpy as jnp
from jax import lax
from jax.sharding import PartitionSpec as P


def shifted(value, axis, by):
    size = lax.axis_size(axis)
    return lax.ppermute(value, axis, [(i, (i + by) % size) for i in range(size)])


def pair_terms(left, right):
    return jnp.einsum("pia,pjb->ijab", left, right, preferred_element_type=jnp.float32)


def flat_amplitudes(flat, pair_energy, pair_live, vir):
    denom = pair_energy[:, None, None] - vir[None, :, None] - vir[None, None, :]
    ampl = flat / denom
    twice = 2.0 * ampl - jnp.swapaxes(ampl, 1, 2)
    return (twice * pair_live[:, None, None]).astype(jnp.bfloat16)


def pair_tables(occ_rows, occ_cols, live_rows, live_cols):
    pair_energy = (occ_rows[:, None] + occ_cols[None, :]).reshape(-1)
    pair_live = (live_rows[:, None] * live_cols[None, :]).reshape(-1)
    return (pair_energy, pair_live)


def on_device(b_tensor, occ_energy, vir_energy, occ_count):
    per_dev = b_tensor.shape[1]
    vpanel = b_tensor.shape[2]
    groups = lax.axis_size("occ")
    half = groups // 2
    here = lax.axis_index("occ")
    mate = (here + half) % groups
    slots = jnp.arange(per_dev, dtype=jnp.int32)
    e_own = lax.dynamic_slice_in_dim(occ_energy, here * per_dev, per_dev)
    e_other = lax.dynamic_slice_in_dim(occ_energy, mate * per_dev, per_dev)
    l_own = (slots < occ_count[here]).astype(jnp.float32)
    l_other = (slots < occ_count[mate]).astype(jnp.float32)
    other = shifted(b_tensor, "occ", half)
    rows_b, cols_b = (b_tensor, other)
    e_rows, e_cols, l_rows, l_cols = (e_own, e_other, l_own, l_other)
    k_diag = pair_terms(b_tensor, b_tensor)
    k_cross = pair_terms(rows_b, cols_b)
    diag_energy, diag_live = pair_tables(e_own, e_own, l_own, l_own)
    cross_energy, cross_live = pair_tables(e_rows, e_cols, l_rows, l_cols)
    flat_diag = k_diag.reshape(-1, vpanel, vpanel)
    flat_cross = k_cross.reshape(-1, vpanel, vpanel)
    flat_diag, flat_cross = lax.psum((flat_diag, flat_cross), "aux")
    t_diag = flat_amplitudes(flat_diag, diag_energy, diag_live, vir_energy)
    t_cross = flat_amplitudes(flat_cross, cross_energy, cross_live, vir_energy)
    t_diag = t_diag.reshape(k_diag.shape)
    t_cross = t_cross.reshape(k_cross.shape)
    total = jnp.einsum("pjb,ijab->pia", b_tensor, t_diag, preferred_element_type=jnp.float32)
    total = total + jnp.einsum("pjb,ijab->pia", other, t_cross, preferred_element_type=jnp.float32)
    return total.astype(jnp.bfloat16)


def solution(mesh):
    return jax.shard_map(
        on_device,
        mesh=mesh,
        in_specs=(P("aux", "occ", None), P(), P(), P()),
        out_specs=P("aux", "occ", None),
        check_vma=False,
    )
```

profile of v0, /device:TPU:1, one launch (start us, length us, event | category | flops | bytes accessed | tf_op | source)
XLA Modules:
  0.0 271.6 jit_solution(16767857078115118869)
XLA Ops:
  6.5 6.3 %copy.16 = bf16[6000,4,128]{2,0,1:T(8,128)(2,1)} copy(bf16[6000,4,128]{2,1,0:T(4,128)(2,1)} %param.4) | data formatting | bytes 12288000 | tf_op args[0]
  12.9 3.6 %collective-permute-start = (bf16[6000,4,128]{2,0,1:T(8,128)(2,1)}, bf16[6000,4,128]{2,0,1:T(8,128)(2,1)}, u32[]{:S(2)}, u32[]{:S(2)}) collective-permute-start(bf16[6000,4,128]{2,0,1:T(8,128)(2,1)} %copy.16), channel_id=1, source_target_pairs={{0,128},{4,132},{8,136},{12,140},{16,144},{20,148},{24,152},{28,15... | collective-permute-start | bytes 18432008 | tf_op jit(solution)/shard_map/ppermute | solution.py:9
  16.5 3.4 %fusion.11 = f32[4,4,128,128]{2,3,0,1:T(8,128)S(1)} fusion(bf16[6000,4,128,1]{2,1,0,3:T(4,128)(2,1)S(1)} %bitcast.61, bf16[6000,4,128]{2,1,0:T(4,128)(2,1)S(1)} %copy-done), kind=kOutput, calls=%fused_computation.12 | convolution fusion | flops 3145728000 | bytes 13336576 | tf_op jit(solution)/shard_map/pia,pjb->ijab/dot_general | solution.py:13
  19.9 1.4 copy.17
  21.3 126.5 %collective-permute-done = bf16[6000,4,128]{2,0,1:T(8,128)(2,1)} collective-permute-done((bf16[6000,4,128]{2,0,1:T(8,128)(2,1)}, bf16[6000,4,128]{2,0,1:T(8,128)(2,1)}, u32[]{:S(2)}, u32[]{:S(2)}) %collective-permute-start) | collective-permute-done | bytes 6144032 | tf_op jit(solution)/shard_map/ppermute | solution.py:9
  147.8 7.3 %fusion.16 = f32[4,4,128,128]{2,3,0,1:T(8,128)S(1)} fusion(bf16[6000,4,128]{2,0,1:T(8,128)(2,1)} %collective-permute-done, bf16[6000,4,128]{2,1,0:T(4,128)(2,1)} %param.4), kind=kOutput, calls=%fused_computation.13 | convolution fusion | flops 3145728000 | bytes 13336576 | tf_op jit(solution)/shard_map/pia,pjb->ijab/dot_general | solution.py:13
  155.1 1.3 copy.23
  156.5 0.7 fusion.29
  157.2 0.6 compare_convert_fusion.1
  157.7 0.7 compare_convert_fusion
  158.5 0.1 mul.71
  158.6 0.1 mul.78
  158.7 0.1 fusion.28
  158.7 0.1 broadcast_add_fusion.1
  158.8 0.1 add.69
  158.9 0.1 add.76
  159.1 65.4 %all-reduce.3.cloned.1.call-done = (f32[16,128,128]{2,1,0:T(8,128)}, f32[16,128,128]{2,1,0:T(8,128)}) async-done(((f32[16,128,128]{2,1,0:T(8,128)}, f32[16,128,128]{2,1,0:T(8,128)}), (f32[16,128,128]{2,1,0:T(8,128)}, f32[16,128,128]{2,1,0:T(8,128)})) %all-reduce.3.cloned.1.call-update) | async-done | bytes 2097168 | tf_op jit(solution)/shard_map/psum | solution.py:50
  224.5 1.9 subtract_divide_fusion.1
  226.4 0.3 copy.18
  226.8 1.3 copy.24
  228.1 1.5 fusion.22
  229.6 5.5 %fusion.6 = f32[4,128,6000,1]{1,2,3,0:T(8,128)S(1)} fusion(bf16[4,4,128,128]{2,3,1,0:T(8,128)(2,1)S(1)} %bitcast.65, bf16[6000,4,128]{2,1,0:T(4,128)(2,1)} %param.4), kind=kOutput, calls=%fused_computation.7 | convolution fusion | flops 3145728000 | bytes 18956288 | tf_op jit(solution)/shard_map/pjb,ijab->pia/dot_general | solution.py:55
  235.1 6.5 %fusion.1 = bf16[6000,4,128]{2,0,1:T(8,128)(2,1)S(1)} fusion(bf16[4,4,128,128]{2,3,1,0:T(8,128)(2,1)S(1)} %bitcast.64, f32[4,128,6000,1]{1,2,3,0:T(8,128)S(1)} %fusion.6, bf16[6000,4,128]{2,0,1:T(8,128)(2,1)} %collective-permute-done), kind=kOutput, calls=%fused_computation.2 | convolution fusion | flops 3151872000 | bytes 25100288 | tf_op jit(solution)/shard_map/pjb,ijab->pia/dot_general | solution.py:56
  241.6 23.2 %copy.26 = bf16[6000,4,128]{2,1,0:T(4,128)(2,1)} copy(bf16[6000,4,128]{2,0,1:T(8,128)(2,1)S(1)} %fusion.1) | data formatting | bytes 12288000 | tf_op jit(solution)/shard_map/convert_element_type | solution.py:57
  (12 shorter events, 0.2 us)
Async XLA Ops:
  6.5 218.0 %all-reduce.3.cloned.1.call-start = ((), (), s32[]{:S(2)}) async-start(), calls=%async_computation | async-start | bytes 4194304 | tf_op jit(solution)/shard_map/psum | solution.py:50
  6.5 9.9 %copy-start = (bf16[6000,4,128]{2,1,0:T(4,128)(2,1)S(1)}, bf16[6000,4,128]{2,1,0:T(4,128)(2,1)}, u32[]{:S(2)}) copy-start(bf16[6000,4,128]{2,1,0:T(4,128)(2,1)} %param.4) | copy-start | bytes 18432004
  12.9 134.9 %collective-permute-start = (bf16[6000,4,128]{2,0,1:T(8,128)(2,1)}, bf16[6000,4,128]{2,0,1:T(8,128)(2,1)}, u32[]{:S(2)}, u32[]{:S(2)}) collective-permute-start(bf16[6000,4,128]{2,0,1:T(8,128)(2,1)} %copy.16), channel_id=1, source_target_pairs={{0,128},{4,132},{8,136},{12,140},{16,144},{20,148},{24,152},{28,15... | collective-permute-start | bytes 18432008 | tf_op jit(solution)/shard_map/ppermute | solution.py:9
  21.3 135.2 %copy-start.2 = (s32[64]{0:T(128)S(1)}, s32[64]{0:T(128)}, u32[]{:S(2)}) copy-start(s32[64]{0:T(128)} %param.7) | copy-start | bytes 772
  21.3 137.4 %copy-start.3 = (f32[256]{0:T(256)S(1)}, f32[256]{0:T(256)}, u32[]{:S(2)}) copy-start(f32[256]{0:T(256)} %param.5) | copy-start | bytes 3076
  21.3 137.7 %copy-start.1 = (f32[128]{0:T(128)S(1)}, f32[128]{0:T(128)}, u32[]{:S(2)}) copy-start(f32[128]{0:T(128)} %param.6) | copy-start | bytes 1540
Sparse Core Ops, SparseCore 0:
  156.6 67.8 all-reduce.2
where the time goes:
time: 272 us
  waiting for transfers between devices  192 us (71%)
  local copies, waits for them, and re-layouts  34.9 us (13%)
  matrix products  22.8 us (8%)
  between operations  13.5 us (5%)
  other arithmetic  4.93 us (2%)
  starting transfers between devices  3.58 us (1%)
    ppermute x1, waiting for transfers between devices, shifted(): lax.ppermute(value, axis, [(i, (i + by) % size) for i in range(size)])  127 us
    psum x1, waiting for transfers between devices, on_device(): flat_diag, flat_cross = lax.psum((flat_diag, flat_cross), 'aux')  65.4 us
    convert_element_type x1, local copies, waits for them, and re-layouts, on_device(): return total.astype(jnp.bfloat16)  23.2 us
    dot_general x2, matrix products, pair_terms(): jnp.einsum('pia,pjb->ijab', left, right, preferred_element_type=jnp.float32)  10.8 us
    dot_general x1, matrix products, on_device(): jnp.einsum('pjb,ijab->pia', other, t_cross, preferred_element_type=jnp.fl...  6.49 us
    unnamed x9, local copies, waits for them, and re-layouts  6.35 us
    dot_general x1, matrix products, on_device(): jnp.einsum('pjb,ijab->pia', b_tensor, t_diag, preferred_element_type=jnp....  5.5 us
  transfers between devices with their start and end apart: 2, of which 2 were waited for; matrix products, arithmetic and copies ran while one was open for 3% of the time, Pallas kernels for 0%

commit v1 on v0

v1 whole, which is shorter than its diff:
```python
import functools

import jax
import jax.numpy as jnp
from jax import lax
from jax.experimental import pallas as pl
from jax.experimental.pallas import tpu as pltpu
from jax.sharding import PartitionSpec as P

CHUNKS = 9
AHEAD = 2
MESH = pl.DeviceIdType.MESH
F32, BF16 = jnp.float32, jnp.bfloat16
KSEND = jnp.float32


def kernel(dims, occ_energy, occ_count, vir, b, out, raw, wide, own, met, far, res, kd, kx, kd_rc, kx_rc,
           kd_out, kd_ri, kx_out, kx_rq, td, tx, tq, blk, load_sem, hop1_s, hop1_r, hop2_s, hop2_r, out_sem,
           ks, kr):
    n_occ, rows, nv, slots = dims
    flat = slots * nv
    half = rows // 2
    size = met.shape[1] // CHUNKS
    start1 = rows - size * CHUNKS
    over = size * CHUNKS - start1
    hv = flat // 2
    o, u = lax.axis_index("occ"), lax.axis_index("aux")
    blocks = n_occ // 2
    h, col = o // blocks, o % blocks
    lo, s = u // 2, u % 2
    x = 2 * h + lo
    u_in = (u + 2) % 4
    other = (o + blocks) % n_occ
    core = (o, u + 1 - 2 * s)
    inner, outer, diag = (o, u_in), (other, u_in), (other, u)

    barrier = pltpu.get_barrier_semaphore()
    for dev in ((o, u_in), (other, u_in), (other, u), core):
        pl.semaphore_signal(barrier, inc=1, device_id=dev, device_id_type=MESH)

    def load(q, c):
        at = slots * (q * start1 + c * size)
        return pltpu.make_async_copy(b.at[pl.ds(at, slots * size)], raw.at[q, c], load_sem.at[q, c])

    for c in range(CHUNKS):
        for q in range(2):
            load(q, c).start()

    def remote(src, dst, ss, rs, dev):
        return pltpu.make_async_remote_copy(src_ref=src, dst_ref=dst, send_sem=ss, recv_sem=rs, device_id=dev,
                                            device_id_type=MESH)

    def at(c):
        return pl.ds(pl.multiple_of(c * size, 16), size)

    def hop1(q, c):
        return remote(own.at[q, at(c)], met.at[h, at(c)], hop1_s.at[q, c], hop1_r.at[h, c],
                      (col + blocks * q, u_in))

    def hop2(t, c):
        return remote(met.at[t, at(c)], far.at[h, at(c)], hop2_s.at[t, c], hop2_r.at[h, c],
                      (col + blocks * (1 - t), u_in))

    def met_wait(c):
        for t in range(2):
            remote(met.at[t, at(c)], met.at[t, at(c)], hop1_s.at[t, c], hop1_r.at[t, c], inner).wait_recv()

    def far_wait(c):
        for t in range(2):
            remote(far.at[t, at(c)], far.at[t, at(c)], hop2_s.at[t, c], hop2_r.at[t, c], inner).wait_recv()

    def flatten(q, c):
        load(q, c).wait()
        wide[q] = raw[q, c].astype(F32)
        for i in range(slots):
            own[q, at(c), i * nv:(i + 1) * nv] = wide[q, pl.ds(i, size, stride=slots), :].astype(BF16)

    flatten(0, 0)
    flatten(1, 0)
    pl.semaphore_wait(barrier, 4)
    for q in range(2):
        hop1(q, 0).start()

    @pl.loop(1, AHEAD)
    def _(c):
        for q in range(2):
            flatten(q, c)
            hop1(q, c).start()

    @pl.loop(AHEAD, CHUNKS)
    def _(c):
        for q in range(2):
            flatten(q, c)

    def gram(lhs, rhs):
        return lax.dot_general(lhs, rhs, (((0,), (0,)), ((), ())), preferred_element_type=F32)

    row = lax.broadcasted_iota(jnp.int32, (size, 1), 0)

    kd[...] = jnp.zeros_like(kd)

    @pl.loop(0, CHUNKS)
    def _(c):
        kd[...] += gram(own[0, at(c)], own[0, at(c)])

    first = own[1, at(0)]
    kd[...] += gram(jnp.where(row >= over, first, jnp.zeros_like(first)), first)

    @pl.loop(1, CHUNKS)
    def _(c):
        kd[...] += gram(own[1, at(c)], own[1, at(c)])

    def half_at(w):
        return pl.ds(pl.multiple_of(w * hv, hv), hv)

    def strip_at(w):
        return pl.ds(pl.multiple_of(w * nv, nv), nv)

    kd_core = remote(kd.at[half_at(1 - s)], kd_rc, ks.at[0], kr.at[0], core)
    kd_core.start()

    vr = jnp.broadcast_to(vir[...], (nv, nv))
    vc = vr.T

    def amplitudes(m, row_occ, row_slot, col_occ, col_slot):
        energy = occ_energy[col_occ * slots + col_slot] + occ_energy[row_occ * slots + row_slot]
        live = (jnp.where(col_slot < occ_count[col_occ], 1.0, 0.0) *
                jnp.where(row_slot < occ_count[row_occ], 1.0, 0.0))
        t = m / ((energy - vr) - vc)
        return (2.0 * t - t.T) * live

    def cross(c):
        lhs, rhs = met[1, at(c)], met[0, at(c)]
        lhs = jnp.where(row + c * size >= over * h, lhs, jnp.zeros_like(lhs))
        kx[...] += gram(lhs, rhs)

    def send(item):
        @pl.when(item < CHUNKS)
        def _():
            for q in range(2):
                hop1(q, item).start()

        @pl.when(item >= CHUNKS)
        def _():
            for t in range(2):
                hop2(t, item - CHUNKS).start()

    kx[...] = jnp.zeros_like(kx)

    def met_step(c):
        met_wait(c)
        send(c + AHEAD)
        cross(c)

    met_step(0)
    kd_core.wait()
    kd_out[...] = (kd[pl.ds(pl.multiple_of(s * hv + (1 - lo) * nv, nv), nv)] + kd_rc[strip_at(1 - lo)]).astype(KSEND)
    kd_inner = remote(kd_out, kd_ri, ks.at[1], kr.at[1], inner)
    kd_inner.start()
    pl.loop(1, 4)(met_step)
    kd_inner.wait()
    mine = 2 * s + lo
    for i in range(slots):
        w = slice(i * nv, (i + 1) * nv)
        m = kd[strip_at(mine), w] + kd_rc[strip_at(lo), w] + kd_ri[:, w].astype(F32)
        td[strip_at(mine), w] = amplitudes(m, o, mine, o, i).astype(BF16)
    td_inner = remote(td.at[strip_at(mine)], td.at[strip_at(mine)], ks.at[2], kr.at[2], inner)
    td_inner.start()
    pl.loop(4, 7)(met_step)
    td_inner.wait()
    td_core = remote(td.at[half_at(s)], td.at[half_at(s)], ks.at[3], kr.at[3], core)
    td_core.start()
    pl.loop(7, CHUNKS)(met_step)

    kx_core = remote(kx.at[half_at(1 - s)], kx_rc, ks.at[4], kr.at[4], core)
    kx_core.start()
    kx_core.wait()
    for p in range(4):
        w = slice((p % 2) * hv, (p % 2 + 1) * hv)
        k = kx[pl.ds(pl.multiple_of(s * hv + (p // 2) * nv, nv), nv), w] + kx_rc[(p // 2) * nv:(p // 2 + 1) * nv, w]
        kx_out[p] = k.astype(KSEND)
        kx[pl.ds(pl.multiple_of((1 - s) * hv + (p // 2) * nv, nv), nv), w] = k
    quarters = []
    for n, (dev, p) in enumerate(((inner, 2 * h + 1 - lo), (outer, 2 * (1 - h) + 1 - lo), (diag, 2 * (1 - h) + lo))):
        quarters.append(remote(kx_out.at[p], kx_rq.at[n], ks.at[5 + n], kr.at[5 + n], dev))
        quarters[-1].start()
    far_wait(0)
    send(CHUNKS + AHEAD)
    for q in quarters:
        q.wait()
    m = kx_rq[0].astype(F32) + kx_rq[1].astype(F32) + kx_rq[2].astype(F32)
    m = m + kx[pl.ds(pl.multiple_of((1 - s) * hv + h * nv, nv), nv), pl.ds(pl.multiple_of(lo * hv, hv), hv)]
    occ_k, occ_m = col, col + blocks
    for i in range(2):
        t = amplitudes(m[:, i * nv:(i + 1) * nv], occ_m, 2 * s + h, occ_k, 2 * lo + i)
        tq[0, i] = t.astype(BF16)
        tq[1, i] = t.T.astype(BF16)
    blk[s, x] = tq[h]
    spread = []
    for n, (dev, to) in enumerate(((inner, h), (outer, 1 - h), (diag, 1 - h))):
        spread.append(remote(tq.at[to], blk.at[s, x], ks.at[8 + n], kr.at[8 + n], dev))
        spread[-1].start()
    far_wait(1)
    send(CHUNKS + AHEAD + 1)
    for q in spread:
        q.wait()
    tx_core = remote(blk.at[s], blk.at[s], ks.at[11], kr.at[11], core)
    tx_core.start()
    far_wait(2)
    send(CHUNKS + AHEAD + 2)
    tx_core.wait()
    td_core.wait()

    def tile(w):
        return slice(w * nv, (w + 1) * nv)

    @pl.when(h == 0)
    def _():
        for ss in range(2):
            for xx in range(4):
                for i in range(2):
                    tx[tile(2 * ss + xx // 2), tile(2 * (xx % 2) + i)] = blk[ss, xx, i]

    @pl.when(h == 1)
    def _():
        for ss in range(2):
            for xx in range(4):
                for i in range(2):
                    tx[tile(2 * (xx % 2) + i), tile(2 * ss + xx // 2)] = blk[ss, xx, i]

    def store(q, c, skip=0):
        at_row = slots * (q * start1 + c * size + skip)
        n = slots * (size - skip)
        return pltpu.make_async_copy(res.at[q, c, pl.ds(slots * skip, n)], out.at[pl.ds(at_row, n)], out_sem.at[q, c])

    def gamma(c, q):
        g = jnp.dot(own[q, at(c)], td[...], preferred_element_type=F32)
        g = g + jnp.dot(far[q, at(c)], tx[...], preferred_element_type=F32)
        for i in range(slots):
            wide[q, pl.ds(i, size, stride=slots), :] = g[:, i * nv:(i + 1) * nv]
        res[q, c] = wide[q].astype(BF16)

    gamma(0, 0)
    store(0, 0).start()
    gamma(0, 1)
    store(1, 0, over).start()

    @pl.loop(1, 3)
    def _(c):
        for q in range(2):
            gamma(c, q)
            store(q, c).start()

    @pl.loop(3, CHUNKS)
    def _(c):
        far_wait(c)

        @pl.when(c + AHEAD < CHUNKS)
        def _():
            for t in range(2):
                hop2(t, c + AHEAD).start()

        for q in range(2):
            gamma(c, q)
            store(q, c).start()

    @pl.loop(0, CHUNKS)
    def _(c):
        for q in range(2):
            hop1(q, c).wait_send()
            hop2(q, c).wait_send()
    store(0, 0).wait()
    store(1, 0, over).wait()

    @pl.loop(1, CHUNKS)
    def _(c):
        for q in range(2):
            store(q, c).wait()


def half_rows(rows):
    unit = 16 * CHUNKS
    return -(-(rows // 2) // unit) * unit


def on_device(b_tensor, occ_energy, vir_energy, occ_count):
    rows, slots, nv = b_tensor.shape
    flat = slots * nv
    nh = half_rows(rows)
    size = nh // CHUNKS
    dims = (lax.axis_size("occ"), rows, nv, slots)
    smem, vmem, hbm = (pl.BlockSpec(memory_space=m) for m in (pltpu.SMEM, pltpu.VMEM, pl.ANY))
    out = pl.pallas_call(
        functools.partial(kernel, dims),
        out_shape=jax.ShapeDtypeStruct((rows * slots, nv), BF16),
        in_specs=[smem, smem, vmem, hbm],
        out_specs=hbm,
        scratch_shapes=[
            pltpu.VMEM((2, CHUNKS, slots * size, nv), BF16),
            pltpu.VMEM((2, slots * size, nv), F32),
            pltpu.VMEM((2, nh, flat), BF16),
            pltpu.VMEM((2, nh, flat), BF16),
            pltpu.VMEM((2, nh, flat), BF16),
            pltpu.VMEM((2, CHUNKS, slots * size, nv), BF16),
            pltpu.VMEM((flat, flat), F32),
            pltpu.VMEM((flat, flat), F32),
            pltpu.VMEM((flat // 2, flat), F32),
            pltpu.VMEM((flat // 2, flat), F32),
            pltpu.VMEM((nv, flat), KSEND),
            pltpu.VMEM((nv, flat), KSEND),
            pltpu.VMEM((4, nv, flat // 2), KSEND),
            pltpu.VMEM((3, nv, flat // 2), KSEND),
            pltpu.VMEM((flat, flat), BF16),
            pltpu.VMEM((flat, flat), BF16),
            pltpu.VMEM((2, 2, nv, nv), BF16),
            pltpu.VMEM((2, 4, 2, nv, nv), BF16),
            pltpu.SemaphoreType.DMA((2, CHUNKS)),
            pltpu.SemaphoreType.DMA((2, CHUNKS)),
            pltpu.SemaphoreType.DMA((2, CHUNKS)),
            pltpu.SemaphoreType.DMA((2, CHUNKS)),
            pltpu.SemaphoreType.DMA((2, CHUNKS)),
            pltpu.SemaphoreType.DMA((2, CHUNKS)),
            pltpu.SemaphoreType.DMA((12,)),
            pltpu.SemaphoreType.DMA((12,)),
        ],
        compiler_params=pltpu.CompilerParams(collective_id=0, has_side_effects=True, vmem_limit_bytes=56 << 20),
    )(occ_energy, occ_count, vir_energy.reshape(1, nv), b_tensor.reshape(rows * slots, nv))
    return out.reshape(rows, slots, nv)


def solution(mesh):
    return jax.shard_map(
        on_device,
        mesh=mesh,
        in_specs=(P("aux", "occ", None), P(), P(), P()),
        out_specs=P("aux", "occ", None),
        check_vma=False,
    )
```

time: 272 us -> 165 us (0.61)
  waiting for transfers between devices: 192 us -> 0 us
  Pallas kernels: 0 us -> 157 us
  local copies, waits for them, and re-layouts: 34.9 us -> 7.52 us
  matrix products: 22.8 us -> 0 us
  between operations: 13.5 us -> 0.01 us
  other arithmetic: 4.93 us -> 0 us
  starting transfers between devices: 3.58 us -> 0 us
    pallas_call x0 -> x1, Pallas kernels: none -> 157 us  [on_device(): pl.pallas_call(functools.partial(kernel, dims), out_shape=jax.ShapeDtypeS...]
    ppermute x1 -> x0, waiting for transfers between devices: 127 us -> none  [shifted(): lax.ppermute(value, axis, [(i, (i + by) % size) for i in range(size)])]
    psum x1 -> x0, waiting for transfers between devices: 65.4 us -> none  [on_device(): flat_diag, flat_cross = lax.psum((flat_diag, flat_cross), 'aux')]
    convert_element_type x1 -> x0, local copies, waits for them, and re-layouts: 23.2 us -> none  [on_device(): return total.astype(jnp.bfloat16)]
    dot_general x4 -> x0, matrix products: 22.8 us -> none  [the longest x2 10.8 us: pair_terms(): jnp.einsum('pia,pjb->ijab', left, right, preferred_element_type=jnp.float32)]
    ppermute x1 -> x0, starting transfers between devices: 3.57 us -> none  [shifted(): lax.ppermute(value, axis, [(i, (i + by) % size) for i in range(size)])]
    convert_element_type x3 -> x0, other arithmetic: 2.79 us -> none  [the longest x1 1.53 us: flat_amplitudes(): return (twice * pair_live[:, None, None]).astype(jnp.bfloat16)]
    unnamed x9 -> x1, local copies, waits for them, and re-layouts: 6.35 us -> 7.52 us
  transfers between devices with their start and end apart: 2 -> 0, of which waited for: 2 -> 0; matrix products, arithmetic and copies ran while one was open for 3% -> 0% of each run, Pallas kernels for 0% -> 0%
where the time goes in v1:
time: 165 us
  Pallas kernels  157 us (95%)
  local copies, waits for them, and re-layouts  7.52 us (5%)
    pallas_call x1, Pallas kernels, on_device(): pl.pallas_call(functools.partial(kernel, dims), out_shape=jax.ShapeDtypeS...  157 us
    unnamed x1, local copies, waits for them, and re-layouts  7.52 us

profile of v1, /device:TPU:1, one launch (start us, length us, event | category | flops | bytes accessed | tf_op | source)
XLA Modules:
  0.0 164.5 jit_solution(3492362667328241191)
XLA Ops:
  0.0 157.0 %shard_map.46 = bf16[24000,128]{1,0:T(8,128)(2,1)} custom-call(f32[256]{0:T(256)} %occ_energy.1, s32[64]{0:T(128)} %occ_count.1, f32[1,128]{1,0:T(1,128)} %bitcast.5, bf16[24000,128]{1,0:T(8,128)(2,1)} %bitcast.4), custom_call_target="tpu_custom_call" | custom-call | tf_op jit(solution)/shard_map/pallas_call | solution.py:293
  157.0 7.5 %copy.6 = bf16[6000,4,128]{2,1,0:T(4,128)(2,1)} copy(bf16[6000,4,128]{2,1,0:T(4,128)(2,1)} %bitcast.3) | data formatting | bytes 12288000

commit v2 on v1

--- a/solution.py
+++ b/solution.py
@@ -11,11 +11,11 @@
 AHEAD = 2
 MESH = pl.DeviceIdType.MESH
 F32, BF16 = jnp.float32, jnp.bfloat16
-KSEND = jnp.float32
-
-
-def kernel(dims, occ_energy, occ_count, vir, b, out, raw, wide, own, met, far, res, kd, kx, kd_rc, kx_rc,
-           kd_out, kd_ri, kx_out, kx_rq, td, tx, tq, blk, load_sem, hop1_s, hop1_r, hop2_s, hop2_r, out_sem,
+KSEND = jnp.bfloat16
+
+
+def kernel(dims, occ_energy, occ_count, vir, b, out, raw, wide, own, met, far, kd, kx, kd_rc, kx_rc,
+           kd_out, kd_ri, kx_out, kx_rq, td, tx, tq, blk, load_sem, hop1_s, hop1_r, hop2_s, hop2_r,
            ks, kr):
     n_occ, rows, nv, slots = dims
     flat = slots * nv
@@ -228,28 +228,22 @@
                 for i in range(2):
                     tx[tile(2 * (xx % 2) + i), tile(2 * ss + xx // 2)] = blk[ss, xx, i]
 
-    def store(q, c, skip=0):
-        at_row = slots * (q * start1 + c * size + skip)
-        n = slots * (size - skip)
-        return pltpu.make_async_copy(res.at[q, c, pl.ds(slots * skip, n)], out.at[pl.ds(at_row, n)], out_sem.at[q, c])
-
-    def gamma(c, q):
+    def gamma(c, q, skip=0):
         g = jnp.dot(own[q, at(c)], td[...], preferred_element_type=F32)
         g = g + jnp.dot(far[q, at(c)], tx[...], preferred_element_type=F32)
         for i in range(slots):
             wide[q, pl.ds(i, size, stride=slots), :] = g[:, i * nv:(i + 1) * nv]
-        res[q, c] = wide[q].astype(BF16)
+        at_row = slots * (q * start1 + c * size + skip)
+        n = slots * (size - skip)
+        out[pl.ds(pl.multiple_of(at_row, 64), n)] = wide[q, slots * skip:].astype(BF16)
 
     gamma(0, 0)
-    store(0, 0).start()
-    gamma(0, 1)
-    store(1, 0, over).start()
+    gamma(0, 1, over)
 
     @pl.loop(1, 3)
     def _(c):
         for q in range(2):
             gamma(c, q)
-            store(q, c).start()
 
     @pl.loop(3, CHUNKS)
     def _(c):
@@ -262,20 +256,12 @@
 
         for q in range(2):
             gamma(c, q)
-            store(q, c).start()
 
     @pl.loop(0, CHUNKS)
     def _(c):
         for q in range(2):
             hop1(q, c).wait_send()
             hop2(q, c).wait_send()
-    store(0, 0).wait()
-    store(1, 0, over).wait()
-
-    @pl.loop(1, CHUNKS)
-    def _(c):
-        for q in range(2):
-            store(q, c).wait()
 
 
 def half_rows(rows):
@@ -292,16 +278,15 @@
     smem, vmem, hbm = (pl.BlockSpec(memory_space=m) for m in (pltpu.SMEM, pltpu.VMEM, pl.ANY))
     out = pl.pallas_call(
         functools.partial(kernel, dims),
-        out_shape=jax.ShapeDtypeStruct((rows * slots, nv), BF16),
+        out_shape=pltpu.VMEM((rows * slots, nv), BF16),
         in_specs=[smem, smem, vmem, hbm],
-        out_specs=hbm,
+        out_specs=vmem,
         scratch_shapes=[
             pltpu.VMEM((2, CHUNKS, slots * size, nv), BF16),
             pltpu.VMEM((2, slots * size, nv), F32),
             pltpu.VMEM((2, nh, flat), BF16),
             pltpu.VMEM((2, nh, flat), BF16),
             pltpu.VMEM((2, nh, flat), BF16),
-            pltpu.VMEM((2, CHUNKS, slots * size, nv), BF16),
             pltpu.VMEM((flat, flat), F32),
             pltpu.VMEM((flat, flat), F32),
             pltpu.VMEM((flat // 2, flat), F32),
@@ -319,11 +304,10 @@
             pltpu.SemaphoreType.DMA((2, CHUNKS)),
             pltpu.SemaphoreType.DMA((2, CHUNKS)),
             pltpu.SemaphoreType.DMA((2, CHUNKS)),
-            pltpu.SemaphoreType.DMA((2, CHUNKS)),
             pltpu.SemaphoreType.DMA((12,)),
             pltpu.SemaphoreType.DMA((12,)),
         ],
-        compiler_params=pltpu.CompilerParams(collective_id=0, has_side_effects=True, vmem_limit_bytes=56 << 20),
+        compiler_params=pltpu.CompilerParams(collective_id=0, has_side_effects=True, vmem_limit_bytes=44 << 20),
     )(occ_energy, occ_count, vir_energy.reshape(1, nv), b_tensor.reshape(rows * slots, nv))
     return out.reshape(rows, slots, nv)
 

time: 165 us -> 155 us (0.939)
  Pallas kernels: 157 us -> 150 us
  local copies, waits for them, and re-layouts: 7.52 us -> 4.65 us
    pallas_call x1, Pallas kernels: 157 us -> 150 us  [on_device(): pl.pallas_call(functools.partial(kernel, dims), out_shape=pltpu.VMEM((row...]
    unnamed x1 -> x7, local copies, waits for them, and re-layouts: 7.52 us -> 4.65 us
where the time goes in v2:
time: 155 us
  Pallas kernels  150 us (97%)
  local copies, waits for them, and re-layouts  4.65 us (3%)
    pallas_call x1, Pallas kernels, on_device(): pl.pallas_call(functools.partial(kernel, dims), out_shape=pltpu.VMEM((row...  150 us
    unnamed x7, local copies, waits for them, and re-layouts  4.65 us

profile of v2, /device:TPU:1, one launch (start us, length us, event | category | flops | bytes accessed | tf_op | source)
XLA Modules:
  0.0 155.1 jit_solution(1262493378000587020)
XLA Ops:
  0.0 0.0 copy-start
  0.0 0.7 copy-done
  0.7 0.0 copy-start.1
  0.7 0.7 copy-done.1
  1.3 0.0 copy-start.2
  1.3 0.7 copy-done.2
  2.0 150.4 %shard_map.46 = bf16[24000,128]{1,0:T(8,128)(2,1)S(1)} custom-call(f32[256]{0:T(256)S(1)} %copy-done, s32[64]{0:T(128)S(1)} %copy-done.1, f32[1,128]{1,0:T(1,128)S(1)} %bitcast.4, bf16[24000,128]{1,0:T(8,128)(2,1)} %bitcast.5), custom_call_target="tpu_custom_call" | custom-call | tf_op jit(solution)/shard_map/pallas_call | solution.py:279
  152.4 2.7 %copy.6 = bf16[6000,4,128]{2,1,0:T(4,128)(2,1)} copy(bf16[6000,4,128]{2,1,0:T(4,128)(2,1)S(1)} %bitcast.3) | data formatting | bytes 12288000
Async XLA Ops:
  0.0 0.7 copy-start
  0.7 0.7 copy-start.1
  1.3 0.7 copy-start.2

commit v3 on v2

--- a/solution.py
+++ b/solution.py
@@ -8,18 +8,21 @@
 from jax.sharding import PartitionSpec as P
 
 CHUNKS = 9
-AHEAD = 2
+GROUP = 8
+AHEAD = 3
 MESH = pl.DeviceIdType.MESH
 F32, BF16 = jnp.float32, jnp.bfloat16
+CAPS = (4, 5, GROUP)
 KSEND = jnp.bfloat16
 
 
-def kernel(dims, occ_energy, occ_count, vir, b, out, raw, wide, own, met, far, kd, kx, kd_rc, kx_rc,
+def kernel(dims, cap, occ_energy, occ_count, vir, b, out, raw, wide, own, last, met, far, far_last, part, packed, crossed,
+           opened, landed, kd, kx, kd_rc, kx_rc,
            kd_out, kd_ri, kx_out, kx_rq, td, tx, tq, blk, load_sem, hop1_s, hop1_r, hop2_s, hop2_r,
-           ks, kr):
+           ks, kr, es, er):
     n_occ, rows, nv, slots = dims
     flat = slots * nv
-    half = rows // 2
+    most = flat - nv
     size = met.shape[1] // CHUNKS
     start1 = rows - size * CHUNKS
     over = size * CHUNKS - start1
@@ -35,7 +38,13 @@
     inner, outer, diag = (o, u_in), (other, u_in), (other, u)
 
     barrier = pltpu.get_barrier_semaphore()
-    for dev in ((o, u_in), (other, u_in), (other, u), core):
+    member = col % GROUP
+    base, other_base = o - member, other - member
+
+    def mate(d):
+        return (member + d) % GROUP
+
+    for dev in (inner, outer, diag, core, *((base + mate(d), u) for d in range(1, GROUP))):
         pl.semaphore_signal(barrier, inc=1, device_id=dev, device_id_type=MESH)
 
     def load(q, c):
@@ -72,12 +81,13 @@
     def flatten(q, c):
         load(q, c).wait()
         wide[q] = raw[q, c].astype(F32)
-        for i in range(slots):
+        for i in range(slots - 1):
             own[q, at(c), i * nv:(i + 1) * nv] = wide[q, pl.ds(i, size, stride=slots), :].astype(BF16)
+        last[q, at(c)] = wide[q, pl.ds(slots - 1, size, stride=slots), :].astype(BF16)
 
     flatten(0, 0)
     flatten(1, 0)
-    pl.semaphore_wait(barrier, 4)
+    pl.semaphore_wait(barrier, 4 + GROUP - 1)
     for q in range(2):
         hop1(q, 0).start()
 
@@ -92,23 +102,71 @@
         for q in range(2):
             flatten(q, c)
 
+    piece = part.shape[1]
+    per = GROUP // 2
+
+    def piece_start(p):
+        return (p % per) * piece - ((p % per) // (per - 1)) * (per * piece - size * CHUNKS)
+
+    def spread(d):
+        p = mate(d)
+        return remote(last.at[p // per, pl.ds(pl.multiple_of(piece_start(p), 16), piece)], part.at[member],
+                      es.at[0, d], er.at[0, d], (base + p, u))
+
+    def gather(d):
+        return remote(opened.at[d], landed.at[member], es.at[1, d], er.at[1, d], (base + mate(d), u))
+
+    def place(first, j):
+        n = jnp.int32(0)
+        for i in range(GROUP):
+            n = n + jnp.where((i < j) & (occ_count[first + i] == slots), 1, 0)
+        return n
+
+    across = remote(packed, crossed, es.at[0, 0], er.at[0, 0], diag)
+
+    def pack():
+        for d in range(1, GROUP):
+            spread(d).wait()
+        for p in range(cap):
+            pick = jnp.int32(0)
+            for j in range(GROUP):
+                pick = pick + jnp.where((occ_count[base + j] == slots) & (place(base, j) == p), j, 0)
+            packed[p] = part[pick]
+        across.start()
+
+    def unpack():
+        across.wait()
+        for d in range(GROUP):
+            opened[d] = crossed[jnp.minimum(place(other_base, mate(d)), cap - 1)]
+        for d in range(1, GROUP):
+            gather(d).start()
+
+    part[member] = last[member // per, pl.ds(pl.multiple_of(piece_start(member), 16), piece)]
+    for d in range(1, GROUP):
+        spread(d).start()
+
     def gram(lhs, rhs):
         return lax.dot_general(lhs, rhs, (((0,), (0,)), ((), ())), preferred_element_type=F32)
 
     row = lax.broadcasted_iota(jnp.int32, (size, 1), 0)
 
+    def whole(head, tail, q, rows_at):
+        return jnp.concatenate([head[q, rows_at], tail[q, rows_at]], axis=1)
+
     kd[...] = jnp.zeros_like(kd)
 
     @pl.loop(0, CHUNKS)
     def _(c):
-        kd[...] += gram(own[0, at(c)], own[0, at(c)])
-
-    first = own[1, at(0)]
+        mine = whole(own, last, 0, at(c))
+        kd[...] += gram(mine, mine)
+
+    first = whole(own, last, 1, at(0))
     kd[...] += gram(jnp.where(row >= over, first, jnp.zeros_like(first)), first)
 
     @pl.loop(1, CHUNKS)
     def _(c):
-        kd[...] += gram(own[1, at(c)], own[1, at(c)])
+        mine = whole(own, last, 1, at(c))
+        kd[...] += gram(mine, mine)
 
     def half_at(w):
         return pl.ds(pl.multiple_of(w * hv, hv), hv)
@@ -132,7 +190,7 @@
     def cross(c):
         lhs, rhs = met[1, at(c)], met[0, at(c)]
         lhs = jnp.where(row + c * size >= over * h, lhs, jnp.zeros_like(lhs))
-        kx[...] += gram(lhs, rhs)
+        kx[:most, :most] += gram(lhs, rhs)
 
     def send(item):
         @pl.when(item < CHUNKS)
@@ -157,7 +215,9 @@
     kd_out[...] = (kd[pl.ds(pl.multiple_of(s * hv + (1 - lo) * nv, nv), nv)] + kd_rc[strip_at(1 - lo)]).astype(KSEND)
     kd_inner = remote(kd_out, kd_ri, ks.at[1], kr.at[1], inner)
     kd_inner.start()
-    pl.loop(1, 4)(met_step)
+    pl.loop(1, 3)(met_step)
+    pack()
+    met_step(3)
     kd_inner.wait()
     mine = 2 * s + lo
     for i in range(slots):
@@ -170,7 +230,34 @@
     td_inner.wait()
     td_core = remote(td.at[half_at(s)], td.at[half_at(s)], ks.at[3], kr.at[3], core)
     td_core.start()
+    unpack()
     pl.loop(7, CHUNKS)(met_step)
+    landed[member] = opened[0]
+    for d in range(1, GROUP):
+        gather(d).wait()
+    for p in range(GROUP):
+        far_last[p // per, pl.ds(piece_start(p), piece)] = landed[p]
+    piece_row = lax.broadcasted_iota(jnp.int32, (piece, 1), 0)
+
+    def fresh(p):
+        skip = ((p % per) // (per - 1)) * (per * piece - size * CHUNKS) + (p // per) * (1 - (p % per + per - 1) // per) * over
+        v = landed[p]
+        return jnp.where(piece_row >= skip, v, jnp.zeros_like(v))
+
+    @pl.when(h == 0)
+    def _():
+        @pl.loop(0, GROUP)
+        def _(p):
+            rows_at = pl.ds(pl.multiple_of(piece_start(p), 16), piece)
+            kx[most:] += gram(fresh(p), whole(own, last, p // per, rows_at))
+
+    @pl.when(h == 1)
+    def _():
+        @pl.loop(0, GROUP)
+        def _(p):
+            rows_at = pl.ds(pl.multiple_of(piece_start(p), 16), piece)
+            kx[:most, most:] += gram(own[p // per, rows_at], fresh(p))
+
 
     kx_core = remote(kx.at[half_at(1 - s)], kx_rc, ks.at[4], kr.at[4], core)
     kx_core.start()
@@ -229,8 +316,8 @@
                     tx[tile(2 * (xx % 2) + i), tile(2 * ss + xx // 2)] = blk[ss, xx, i]
 
     def gamma(c, q, skip=0):
-        g = jnp.dot(own[q, at(c)], td[...], preferred_element_type=F32)
-        g = g + jnp.dot(far[q, at(c)], tx[...], preferred_element_type=F32)
+        g = jnp.dot(whole(own, last, q, at(c)), td[...], preferred_element_type=F32)
+        g = g + jnp.dot(whole(far, far_last, q, at(c)), tx[...], preferred_element_type=F32)
         for i in range(slots):
             wide[q, pl.ds(i, size, stride=slots), :] = g[:, i * nv:(i + 1) * nv]
         at_row = slots * (q * start1 + c * size + skip)
@@ -276,39 +363,56 @@
     size = nh // CHUNKS
     dims = (lax.axis_size("occ"), rows, nv, slots)
     smem, vmem, hbm = (pl.BlockSpec(memory_space=m) for m in (pltpu.SMEM, pltpu.VMEM, pl.ANY))
-    out = pl.pallas_call(
-        functools.partial(kernel, dims),
-        out_shape=pltpu.VMEM((rows * slots, nv), BF16),
-        in_specs=[smem, smem, vmem, hbm],
-        out_specs=vmem,
-        scratch_shapes=[
-            pltpu.VMEM((2, CHUNKS, slots * size, nv), BF16),
-            pltpu.VMEM((2, slots * size, nv), F32),
-            pltpu.VMEM((2, nh, flat), BF16),
-            pltpu.VMEM((2, nh, flat), BF16),
-            pltpu.VMEM((2, nh, flat), BF16),
-            pltpu.VMEM((flat, flat), F32),
-            pltpu.VMEM((flat, flat), F32),
-            pltpu.VMEM((flat // 2, flat), F32),
-            pltpu.VMEM((flat // 2, flat), F32),
-            pltpu.VMEM((nv, flat), KSEND),
-            pltpu.VMEM((nv, flat), KSEND),
-            pltpu.VMEM((4, nv, flat // 2), KSEND),
-            pltpu.VMEM((3, nv, flat // 2), KSEND),
-            pltpu.VMEM((flat, flat), BF16),
-            pltpu.VMEM((flat, flat), BF16),
-            pltpu.VMEM((2, 2, nv, nv), BF16),
-            pltpu.VMEM((2, 4, 2, nv, nv), BF16),
-            pltpu.SemaphoreType.DMA((2, CHUNKS)),
-            pltpu.SemaphoreType.DMA((2, CHUNKS)),
-            pltpu.SemaphoreType.DMA((2, CHUNKS)),
-            pltpu.SemaphoreType.DMA((2, CHUNKS)),
-            pltpu.SemaphoreType.DMA((2, CHUNKS)),
-            pltpu.SemaphoreType.DMA((12,)),
-            pltpu.SemaphoreType.DMA((12,)),
-        ],
-        compiler_params=pltpu.CompilerParams(collective_id=0, has_side_effects=True, vmem_limit_bytes=44 << 20),
-    )(occ_energy, occ_count, vir_energy.reshape(1, nv), b_tensor.reshape(rows * slots, nv))
+    piece = -(-nh // (GROUP // 2) // 16) * 16
+
+    def run(number, cap):
+        return pl.pallas_call(
+            functools.partial(kernel, dims, cap),
+            out_shape=pltpu.VMEM((rows * slots, nv), BF16),
+            in_specs=[smem, smem, vmem, hbm],
+            out_specs=vmem,
+            scratch_shapes=[
+                pltpu.VMEM((2, CHUNKS, slots * size, nv), BF16),
+                pltpu.VMEM((2, slots * size, nv), F32),
+                pltpu.VMEM((2, nh, flat - nv), BF16),
+                pltpu.VMEM((2, nh, nv), BF16),
+                pltpu.VMEM((2, nh, flat - nv), BF16),
+                pltpu.VMEM((2, nh, flat - nv), BF16),
+                pltpu.VMEM((2, nh, nv), BF16),
+                pltpu.VMEM((GROUP, piece, nv), BF16),
+                pltpu.VMEM((cap, piece, nv), BF16),
+                pltpu.VMEM((cap, piece, nv), BF16),
+                pltpu.VMEM((GROUP, piece, nv), BF16),
+                pltpu.VMEM((GROUP, piece, nv), BF16),
+                pltpu.VMEM((flat, flat), F32),
+                pltpu.VMEM((flat, flat), F32),
+                pltpu.VMEM((flat // 2, flat), F32),
+                pltpu.VMEM((flat // 2, flat), F32),
+                pltpu.VMEM((nv, flat), KSEND),
+                pltpu.VMEM((nv, flat), KSEND),
+                pltpu.VMEM((4, nv, flat // 2), KSEND),
+                pltpu.VMEM((3, nv, flat // 2), KSEND),
+                pltpu.VMEM((flat, flat), BF16),
+                pltpu.VMEM((flat, flat), BF16),
+                pltpu.VMEM((2, 2, nv, nv), BF16),
+                pltpu.VMEM((2, 4, 2, nv, nv), BF16),
+                pltpu.SemaphoreType.DMA((2, CHUNKS)),
+                pltpu.SemaphoreType.DMA((2, CHUNKS)),
+                pltpu.SemaphoreType.DMA((2, CHUNKS)),
+                pltpu.SemaphoreType.DMA((2, CHUNKS)),
+                pltpu.SemaphoreType.DMA((2, CHUNKS)),
+                pltpu.SemaphoreType.DMA((12,)),
+                pltpu.SemaphoreType.DMA((12,)),
+                pltpu.SemaphoreType.DMA((2, GROUP)),
+                pltpu.SemaphoreType.DMA((2, GROUP)),
+            ],
+            compiler_params=pltpu.CompilerParams(collective_id=number, has_side_effects=True,
+                                                 vmem_limit_bytes=46 << 20),
+        )(occ_energy, occ_count, vir_energy.reshape(1, nv), b_tensor.reshape(rows * slots, nv))
+
+    full = (occ_count == slots).astype(jnp.int32).reshape(-1, GROUP).sum(axis=1).max()
+    which = sum((full > cap).astype(jnp.int32) for cap in CAPS[:-1])
+    out = lax.switch(which, [functools.partial(run, n, cap) for n, cap in enumerate(CAPS)])
     return out.reshape(rows, slots, nv)
 
 

time: 155 us -> 144 us (0.929)
  Pallas kernels: 150 us -> 138 us
  local copies, waits for them, and re-layouts: 4.65 us -> 2.74 us
    pallas_call x1, Pallas kernels: 150 us -> 138 us  [run(): pl.pallas_call(functools.partial(kernel, dims, cap), out_shape=pltpu.VMEM...]
    unnamed x7 -> x1, local copies, waits for them, and re-layouts: 4.65 us -> 2.66 us
where the time goes in v3:
time: 144 us; the launch traced here: 143 us
  Pallas kernels  138 us (96%)
  local copies, waits for them, and re-layouts  2.74 us (2%)
    pallas_call x1, Pallas kernels, run(): pl.pallas_call(functools.partial(kernel, dims, cap), out_shape=pltpu.VMEM...  138 us

profile of v3, /device:TPU:1, one launch (start us, length us, event | category | flops | bytes accessed | tf_op | source)
XLA Modules:
  0.0 143.4 jit_solution(10106409267048440445)
XLA Ops:
  0.0 0.7 compare_convert_fusion
  0.7 0.1 reshape.37
  0.7 0.1 reduce_sum.9
  0.9 0.6 reduce_max.9
  2.8 138.0 %conditional.1 = (bf16[6000,4,128]{2,1,0:T(4,128)(2,1)S(1)}) conditional(s32[]{:T(128)} %clamp.3, (f32[128]{0:T(128)}, bf16[6000,4,128]{2,1,0:T(4,128)(2,1)}, f32[256]{0:T(256)}, s32[64]{0:T(128)}) %tuple.17, (f32[128]{0:T(128)}, bf16[6000,4,128]{2,1,0:T(4,128)(2,1)}, f32[256]{0:T(256)}, s32[64]{0:T(128)}) %tuple.17, (f32[128]{0:T(128)}, ...), branch_computations={%region_2.0_spmd, %region_3.0_spmd, %region_4.0_spmd} | conditional | bytes 8 | solution.py:415
  2.8 137.7 %branch_0_fun.1 = bf16[24000,128]{1,0:T(8,128)(2,1)S(1)} custom-call(f32[256]{0:T(256)} %get-tuple-element.62.occ_energy, s32[64]{0:T(128)} %get-tuple-element.35.occ_count, f32[1,128]{1,0:T(1,128)} %bitcast.15, bf16[24000,128]{1,0:T(8,128)(2,1)} %bitcast.12), custom_call_target="tpu_custom_call" | custom-call | tf_op jit(solution)/shard_map/cond/branch_0_fun/pallas_call | solution.py:369
  140.8 2.7 %copy.21 = bf16[6000,4,128]{2,1,0:T(4,128)(2,1)} copy(bf16[6000,4,128]{2,1,0:T(4,128)(2,1)S(1)} %get-tuple-element.46) | data formatting | bytes 12288000

commit v4 on v3

--- a/solution.py
+++ b/solution.py
@@ -12,13 +12,14 @@
 AHEAD = 3
 MESH = pl.DeviceIdType.MESH
 F32, BF16 = jnp.float32, jnp.bfloat16
-CAPS = (4, 5, GROUP)
+CAPS = (3, 4, 5, GROUP)
+STEPS = (0, 5, 2, 6, 8, 7, 8, 9, 10, 11)
 KSEND = jnp.bfloat16
 
 
 def kernel(dims, cap, occ_energy, occ_count, vir, b, out, raw, wide, own, last, met, far, far_last, part, packed, crossed,
            opened, landed, kd, kx, kd_rc, kx_rc,
-           kd_out, kd_ri, kx_out, kx_rq, td, tx, tq, blk, load_sem, hop1_s, hop1_r, hop2_s, hop2_r,
+           kd_out, kd_ri, kx_out, kx_rq, td, tx, tq, blk, kd_up, td_up, load_sem, hop1_s, hop1_r, hop2_s, hop2_r,
            ks, kr, es, er):
     n_occ, rows, nv, slots = dims
     flat = slots * nv
@@ -51,9 +52,8 @@
         at = slots * (q * start1 + c * size)
         return pltpu.make_async_copy(b.at[pl.ds(at, slots * size)], raw.at[q, c], load_sem.at[q, c])
 
-    for c in range(CHUNKS):
-        for q in range(2):
-            load(q, c).start()
+    for q in range(2):
+        load(q, 0).start()
 
     def remote(src, dst, ss, rs, dev):
         return pltpu.make_async_remote_copy(src_ref=src, dst_ref=dst, send_sem=ss, recv_sem=rs, device_id=dev,
@@ -90,6 +90,9 @@
     pl.semaphore_wait(barrier, 4 + GROUP - 1)
     for q in range(2):
         hop1(q, 0).start()
+    for c in range(1, CHUNKS):
+        for q in range(2):
+            load(q, c).start()
 
     @pl.loop(1, AHEAD)
     def _(c):
@@ -114,35 +117,44 @@
                       es.at[0, d], er.at[0, d], (base + p, u))
 
     def gather(d):
-        return remote(opened.at[d], landed.at[member], es.at[1, d], er.at[1, d], (base + mate(d), u))
-
-    def place(first, j):
-        n = jnp.int32(0)
-        for i in range(GROUP):
-            n = n + jnp.where((i < j) & (occ_count[first + i] == slots), 1, 0)
-        return n
+        return remote(opened.at[mate(d)], landed.at[member], es.at[1, d], er.at[1, d], (base + mate(d), u))
+
+    def places(first):
+        n, found = jnp.int32(0), []
+        for j in range(GROUP):
+            one = jnp.where(occ_count[first + j] == slots, 1, 0)
+            found.append((one, n))
+            n = n + one
+        return found
 
     across = remote(packed, crossed, es.at[0, 0], er.at[0, 0], diag)
 
     def pack():
-        for d in range(1, GROUP):
+        @pl.loop(1, GROUP)
+        def _(d):
             spread(d).wait()
+
+        found = places(base)
         for p in range(cap):
             pick = jnp.int32(0)
-            for j in range(GROUP):
-                pick = pick + jnp.where((occ_count[base + j] == slots) & (place(base, j) == p), j, 0)
+            for j, (one, n) in enumerate(found):
+                pick = pick + jnp.where(n == p, one * j, 0)
             packed[p] = part[pick]
         across.start()
 
     def unpack():
         across.wait()
-        for d in range(GROUP):
-            opened[d] = crossed[jnp.minimum(place(other_base, mate(d)), cap - 1)]
-        for d in range(1, GROUP):
+        for j, (_, n) in enumerate(places(other_base)):
+            opened[j] = crossed[jnp.minimum(n, cap - 1)]
+
+        @pl.loop(1, GROUP)
+        def _(d):
             gather(d).start()
 
     part[member] = last[member // per, pl.ds(pl.multiple_of(piece_start(member), 16), piece)]
-    for d in range(1, GROUP):
+
+    @pl.loop(1, GROUP)
+    def _(d):
         spread(d).start()
 
     def gram(lhs, rhs):
@@ -168,13 +180,18 @@
         mine = whole(own, last, 1, at(c))
         kd[...] += gram(mine, mine)
 
+    def tile(w):
+        return slice(w * nv, (w + 1) * nv)
+
+    upper = [(j, i) for j in range(slots) for i in range(j, slots)]
+    split = len(upper) // 2
+    for n, (j, i) in enumerate(upper):
+        kd_up[n // split, n % split] = kd[tile(j), tile(i)]
+
     def half_at(w):
         return pl.ds(pl.multiple_of(w * hv, hv), hv)
 
-    def strip_at(w):
-        return pl.ds(pl.multiple_of(w * nv, nv), nv)
-
-    kd_core = remote(kd.at[half_at(1 - s)], kd_rc, ks.at[0], kr.at[0], core)
+    kd_core = remote(kd_up.at[1 - s], kd_rc, ks.at[0], kr.at[0], core)
     kd_core.start()
 
     vr = jnp.broadcast_to(vir[...], (nv, nv))
@@ -210,110 +227,136 @@
         send(c + AHEAD)
         cross(c)
 
-    met_step(0)
-    kd_core.wait()
-    kd_out[...] = (kd[pl.ds(pl.multiple_of(s * hv + (1 - lo) * nv, nv), nv)] + kd_rc[strip_at(1 - lo)]).astype(KSEND)
     kd_inner = remote(kd_out, kd_ri, ks.at[1], kr.at[1], inner)
-    kd_inner.start()
-    pl.loop(1, 3)(met_step)
-    pack()
-    met_step(3)
-    kd_inner.wait()
-    mine = 2 * s + lo
-    for i in range(slots):
-        w = slice(i * nv, (i + 1) * nv)
-        m = kd[strip_at(mine), w] + kd_rc[strip_at(lo), w] + kd_ri[:, w].astype(F32)
-        td[strip_at(mine), w] = amplitudes(m, o, mine, o, i).astype(BF16)
-    td_inner = remote(td.at[strip_at(mine)], td.at[strip_at(mine)], ks.at[2], kr.at[2], inner)
-    td_inner.start()
-    pl.loop(4, 7)(met_step)
-    td_inner.wait()
-    td_core = remote(td.at[half_at(s)], td.at[half_at(s)], ks.at[3], kr.at[3], core)
-    td_core.start()
-    unpack()
-    pl.loop(7, CHUNKS)(met_step)
-    landed[member] = opened[0]
-    for d in range(1, GROUP):
-        gather(d).wait()
-    for p in range(GROUP):
-        far_last[p // per, pl.ds(piece_start(p), piece)] = landed[p]
-    piece_row = lax.broadcasted_iota(jnp.int32, (piece, 1), 0)
-
-    def fresh(p):
-        skip = ((p % per) // (per - 1)) * (per * piece - size * CHUNKS) + (p // per) * (1 - (p % per + per - 1) // per) * over
-        v = landed[p]
-        return jnp.where(piece_row >= skip, v, jnp.zeros_like(v))
-
-    @pl.when(h == 0)
-    def _():
+    td_core = remote(td_up.at[s], td_up.at[s], ks.at[3], kr.at[3], core)
+
+    def diag_send():
+        kd_core.wait()
+        kd_out[...] = (kd_up[s] + kd_rc[...]).astype(KSEND)
+        kd_inner.start()
+
+    def diag_tiles():
+        kd_inner.wait()
+        for n in range(split):
+            (j, i), (jj, ii) = upper[n], upper[n + split]
+            m = kd_up[s, n] + kd_rc[n] + kd_ri[n].astype(F32)
+            td_up[s, n] = amplitudes(m, o, j + s * (jj - j), o, i + s * (ii - i)).astype(BF16)
+        td_core.start()
+
+    def diag_place():
+        td_core.wait()
+        for n, (j, i) in enumerate(upper):
+            t = td_up[n // split, n % split]
+            td[tile(j), tile(i)] = t
+            if j != i:
+                td[tile(i), tile(j)] = t.astype(F32).T.astype(BF16)
+
+    def land():
+        landed[member] = opened[member]
+
+        @pl.loop(1, GROUP)
+        def _(d):
+            gather(d).wait()
+
         @pl.loop(0, GROUP)
         def _(p):
-            rows_at = pl.ds(pl.multiple_of(piece_start(p), 16), piece)
-            kx[most:] += gram(fresh(p), whole(own, last, p // per, rows_at))
-
-    @pl.when(h == 1)
-    def _():
-        @pl.loop(0, GROUP)
-        def _(p):
-            rows_at = pl.ds(pl.multiple_of(piece_start(p), 16), piece)
-            kx[:most, most:] += gram(own[p // per, rows_at], fresh(p))
-
+            far_last[p // per, pl.ds(pl.multiple_of(piece_start(p), 16), piece)] = landed[p]
+
+        big = 3 * size
+        big_row = lax.broadcasted_iota(jnp.int32, (big, 1), 0)
+
+        def fresh(c):
+            v = far_last[c // (CHUNKS // 3), big_at(c)]
+            return jnp.where((big_row >= over) | (c != CHUNKS // 3), v, jnp.zeros_like(v))
+
+        def big_at(c):
+            return pl.ds(pl.multiple_of((c % (CHUNKS // 3)) * big, 16), big)
+
+        @pl.when(h == 0)
+        def _():
+            @pl.loop(0, 2 * CHUNKS // 3)
+            def _(c):
+                kx[most:] += gram(fresh(c), whole(own, last, c // (CHUNKS // 3), big_at(c)))
+
+        @pl.when(h == 1)
+        def _():
+            @pl.loop(0, 2 * CHUNKS // 3)
+            def _(c):
+                kx[:most, most:] += gram(own[c // (CHUNKS // 3), big_at(c)], fresh(c))
 
     kx_core = remote(kx.at[half_at(1 - s)], kx_rc, ks.at[4], kr.at[4], core)
-    kx_core.start()
-    kx_core.wait()
-    for p in range(4):
-        w = slice((p % 2) * hv, (p % 2 + 1) * hv)
-        k = kx[pl.ds(pl.multiple_of(s * hv + (p // 2) * nv, nv), nv), w] + kx_rc[(p // 2) * nv:(p // 2 + 1) * nv, w]
-        kx_out[p] = k.astype(KSEND)
-        kx[pl.ds(pl.multiple_of((1 - s) * hv + (p // 2) * nv, nv), nv), w] = k
-    quarters = []
-    for n, (dev, p) in enumerate(((inner, 2 * h + 1 - lo), (outer, 2 * (1 - h) + 1 - lo), (diag, 2 * (1 - h) + lo))):
-        quarters.append(remote(kx_out.at[p], kx_rq.at[n], ks.at[5 + n], kr.at[5 + n], dev))
-        quarters[-1].start()
-    far_wait(0)
-    send(CHUNKS + AHEAD)
-    for q in quarters:
-        q.wait()
-    m = kx_rq[0].astype(F32) + kx_rq[1].astype(F32) + kx_rq[2].astype(F32)
-    m = m + kx[pl.ds(pl.multiple_of((1 - s) * hv + h * nv, nv), nv), pl.ds(pl.multiple_of(lo * hv, hv), hv)]
-    occ_k, occ_m = col, col + blocks
-    for i in range(2):
-        t = amplitudes(m[:, i * nv:(i + 1) * nv], occ_m, 2 * s + h, occ_k, 2 * lo + i)
-        tq[0, i] = t.astype(BF16)
-        tq[1, i] = t.T.astype(BF16)
-    blk[s, x] = tq[h]
-    spread = []
-    for n, (dev, to) in enumerate(((inner, h), (outer, 1 - h), (diag, 1 - h))):
-        spread.append(remote(tq.at[to], blk.at[s, x], ks.at[8 + n], kr.at[8 + n], dev))
-        spread[-1].start()
-    far_wait(1)
-    send(CHUNKS + AHEAD + 1)
-    for q in spread:
-        q.wait()
+    quarters = [remote(kx_out.at[p], kx_rq.at[n], ks.at[5 + n], kr.at[5 + n], dev) for n, (dev, p) in enumerate(
+        ((inner, 2 * h + 1 - lo), (outer, 2 * (1 - h) + 1 - lo), (diag, 2 * (1 - h) + lo)))]
+    shares = [remote(tq.at[to], blk.at[s, x], ks.at[8 + n], kr.at[8 + n], dev) for n, (dev, to) in enumerate(
+        ((inner, h), (outer, 1 - h), (diag, 1 - h)))]
     tx_core = remote(blk.at[s], blk.at[s], ks.at[11], kr.at[11], core)
-    tx_core.start()
-    far_wait(2)
-    send(CHUNKS + AHEAD + 2)
-    tx_core.wait()
-    td_core.wait()
-
-    def tile(w):
-        return slice(w * nv, (w + 1) * nv)
-
-    @pl.when(h == 0)
-    def _():
-        for ss in range(2):
-            for xx in range(4):
-                for i in range(2):
-                    tx[tile(2 * ss + xx // 2), tile(2 * (xx % 2) + i)] = blk[ss, xx, i]
-
-    @pl.when(h == 1)
-    def _():
-        for ss in range(2):
-            for xx in range(4):
-                for i in range(2):
-                    tx[tile(2 * (xx % 2) + i), tile(2 * ss + xx // 2)] = blk[ss, xx, i]
+
+    def cross_send():
+        kx_core.start()
+        kx_core.wait()
+        for p in range(4):
+            w = slice((p % 2) * hv, (p % 2 + 1) * hv)
+            k = kx[pl.ds(pl.multiple_of(s * hv + (p // 2) * nv, nv), nv), w] + kx_rc[tile(p // 2), w]
+            kx_out[p] = k.astype(KSEND)
+            kx[pl.ds(pl.multiple_of((1 - s) * hv + (p // 2) * nv, nv), nv), w] = k
+        for q in quarters:
+            q.start()
+
+    def cross_tiles():
+        for q in quarters:
+            q.wait()
+        m = kx_rq[0].astype(F32) + kx_rq[1].astype(F32) + kx_rq[2].astype(F32)
+        m = m + kx[pl.ds(pl.multiple_of((1 - s) * hv + h * nv, nv), nv), pl.ds(pl.multiple_of(lo * hv, hv), hv)]
+        occ_k, occ_m = col, col + blocks
+        for i in range(2):
+            t = amplitudes(m[:, i * nv:(i + 1) * nv], occ_m, 2 * s + h, occ_k, 2 * lo + i)
+            tq[0, i] = t.astype(BF16)
+            tq[1, i] = t.T.astype(BF16)
+        blk[s, x] = tq[h]
+        for q in shares:
+            q.start()
+
+    def cross_swap():
+        for q in shares:
+            q.wait()
+        tx_core.start()
+
+    def cross_place():
+        tx_core.wait()
+
+        @pl.when(h == 0)
+        def _():
+            for ss in range(2):
+                for xx in range(4):
+                    for i in range(2):
+                        tx[tile(2 * ss + xx // 2), tile(2 * (xx % 2) + i)] = blk[ss, xx, i]
+
+        @pl.when(h == 1)
+        def _():
+            for ss in range(2):
+                for xx in range(4):
+                    for i in range(2):
+                        tx[tile(2 * (xx % 2) + i), tile(2 * ss + xx // 2)] = blk[ss, xx, i]
+
+    after = {}
+    for step, todo in zip(STEPS, (diag_send, diag_tiles, pack, unpack, land, diag_place, cross_send, cross_tiles,
+                                  cross_swap, cross_place), strict=True):
+        after.setdefault(step, []).append(todo)
+    begin = 0
+    for step in sorted(after):
+        if step < CHUNKS:
+            pl.loop(begin, step + 1)(met_step)
+        else:
+            if begin < CHUNKS:
+                pl.loop(begin, CHUNKS)(met_step)
+            for c in range(max(begin, CHUNKS), step + 1):
+                far_wait(c - CHUNKS)
+                if c + AHEAD < 2 * CHUNKS:
+                    send(c + AHEAD)
+        begin = step + 1
+        for todo in after[step]:
+            todo()
+    ready = begin - CHUNKS
 
     def gamma(c, q, skip=0):
         g = jnp.dot(whole(own, last, q, at(c)), td[...], preferred_element_type=F32)
@@ -327,12 +370,12 @@
     gamma(0, 0)
     gamma(0, 1, over)
 
-    @pl.loop(1, 3)
+    @pl.loop(1, ready)
     def _(c):
         for q in range(2):
             gamma(c, q)
 
-    @pl.loop(3, CHUNKS)
+    @pl.loop(ready, CHUNKS)
     def _(c):
         far_wait(c)
 
@@ -363,6 +406,7 @@
     size = nh // CHUNKS
     dims = (lax.axis_size("occ"), rows, nv, slots)
     smem, vmem, hbm = (pl.BlockSpec(memory_space=m) for m in (pltpu.SMEM, pltpu.VMEM, pl.ANY))
+    half_up = slots * (slots + 1) // 4
     piece = -(-nh // (GROUP // 2) // 16) * 16
 
     def run(number, cap):
@@ -386,16 +430,18 @@
                 pltpu.VMEM((GROUP, piece, nv), BF16),
                 pltpu.VMEM((flat, flat), F32),
                 pltpu.VMEM((flat, flat), F32),
+                pltpu.VMEM((half_up, nv, nv), F32),
                 pltpu.VMEM((flat // 2, flat), F32),
-                pltpu.VMEM((flat // 2, flat), F32),
-                pltpu.VMEM((nv, flat), KSEND),
-                pltpu.VMEM((nv, flat), KSEND),
+                pltpu.VMEM((half_up, nv, nv), KSEND),
+                pltpu.VMEM((half_up, nv, nv), KSEND),
                 pltpu.VMEM((4, nv, flat // 2), KSEND),
                 pltpu.VMEM((3, nv, flat // 2), KSEND),
                 pltpu.VMEM((flat, flat), BF16),
                 pltpu.VMEM((flat, flat), BF16),
                 pltpu.VMEM((2, 2, nv, nv), BF16),
                 pltpu.VMEM((2, 4, 2, nv, nv), BF16),
+                pltpu.VMEM((2, half_up, nv, nv), F32),
+                pltpu.VMEM((2, half_up, nv, nv), BF16),
                 pltpu.SemaphoreType.DMA((2, CHUNKS)),
                 pltpu.SemaphoreType.DMA((2, CHUNKS)),
                 pltpu.SemaphoreType.DMA((2, CHUNKS)),
@@ -410,8 +456,8 @@
                                                  vmem_limit_bytes=46 << 20),
         )(occ_energy, occ_count, vir_energy.reshape(1, nv), b_tensor.reshape(rows * slots, nv))
 
-    full = (occ_count == slots).astype(jnp.int32).reshape(-1, GROUP).sum(axis=1).max()
-    which = sum((full > cap).astype(jnp.int32) for cap in CAPS[:-1])
+    full = (occ_count == slots).astype(jnp.int32).reshape(-1, GROUP).sum(axis=1)
+    which = sum((full > cap).astype(jnp.int32) for cap in CAPS[:-1]).max()
     out = lax.switch(which, [functools.partial(run, n, cap) for n, cap in enumerate(CAPS)])
     return out.reshape(rows, slots, nv)
 

time: 144 us -> 137 us (0.951)
  Pallas kernels: 138 us -> 131 us
    pallas_call x1, Pallas kernels: 138 us -> 131 us  [run(): pl.pallas_call(functools.partial(kernel, dims, cap), out_shape=pltpu.VMEM...]
where the time goes in v4:
time: 137 us
  Pallas kernels  131 us (96%)
  local copies, waits for them, and re-layouts  2.74 us (2%)
  other arithmetic  1.42 us (1%)
    pallas_call x1, Pallas kernels, run(): pl.pallas_call(functools.partial(kernel, dims, cap), out_shape=pltpu.VMEM...  131 us

profile of v4, /device:TPU:1, one launch (start us, length us, event | category | flops | bytes accessed | tf_op | source)
XLA Modules:
  0.0 136.7 jit_solution(2910576199129734507)
XLA Ops:
  0.0 0.7 compare_convert_fusion.3
  0.7 0.1 reshape.46
  0.7 0.1 reduce_sum.9
  0.9 0.6 fusion.2
  2.2 131.8 %conditional.1 = (bf16[6000,4,128]{2,1,0:T(4,128)(2,1)S(1)}) conditional(s32[]{:T(128)} %clamp.3, (f32[128]{0:T(128)}, bf16[6000,4,128]{2,1,0:T(4,128)(2,1)}, f32[256]{0:T(256)}, s32[64]{0:T(128)}) %tuple.21, (f32[128]{0:T(128)}, bf16[6000,4,128]{2,1,0:T(4,128)(2,1)}, f32[256]{0:T(256)}, s32[64]{0:T(128)}) %tuple.21, ...), branch_computations={%region_2.0_spmd, %region_3.0_spmd, %region_4.0_spmd, %region_5.0_... | conditional | bytes 8 | solution.py:461
  2.2 131.3 %branch_0_fun.1 = bf16[24000,128]{1,0:T(8,128)(2,1)S(1)} custom-call(f32[256]{0:T(256)} %get-tuple-element.80.occ_energy, s32[64]{0:T(128)} %get-tuple-element.44.occ_count, f32[1,128]{1,0:T(1,128)} %bitcast.20, bf16[24000,128]{1,0:T(8,128)(2,1)} %bitcast.16), custom_call_target="tpu_custom_call" | custom-call | tf_op jit(solution)/shard_map/cond/branch_0_fun/pallas_call | solution.py:413
  134.0 2.7 %copy.26 = bf16[6000,4,128]{2,1,0:T(4,128)(2,1)} copy(bf16[6000,4,128]{2,1,0:T(4,128)(2,1)S(1)} %get-tuple-element.59) | data formatting | bytes 12288000

commit v5 on v4

--- a/solution.py
+++ b/solution.py
@@ -9,17 +9,17 @@
 
 CHUNKS = 9
 GROUP = 8
-AHEAD = 3
+AHEAD = 4
 MESH = pl.DeviceIdType.MESH
 F32, BF16 = jnp.float32, jnp.bfloat16
 CAPS = (3, 4, 5, GROUP)
-STEPS = (0, 5, 2, 6, 8, 7, 8, 9, 10, 11)
+STEPS = (0, 5, 2, 6, 8, 7, 8, 9, 10, 11, 12, 13)
 KSEND = jnp.bfloat16
 
 
 def kernel(dims, cap, occ_energy, occ_count, vir, b, out, raw, wide, own, last, met, far, far_last, part, packed, crossed,
            opened, landed, kd, kx, kd_rc, kx_rc,
-           kd_out, kd_ri, kx_out, kx_rq, td, tx, tq, blk, kd_up, td_up, load_sem, hop1_s, hop1_r, hop2_s, hop2_r,
+           kd_out, kd_ri, kx_out, kx_ro, kx_half, kx_ri, td, tx, tq, turned, blk, kd_up, td_up, load_sem, hop1_s, hop1_r, hop2_s, hop2_r,
            ks, kr, es, er):
     n_occ, rows, nv, slots = dims
     flat = slots * nv
@@ -285,11 +285,14 @@
                 kx[:most, most:] += gram(own[c // (CHUNKS // 3), big_at(c)], fresh(c))
 
     kx_core = remote(kx.at[half_at(1 - s)], kx_rc, ks.at[4], kr.at[4], core)
-    quarters = [remote(kx_out.at[p], kx_rq.at[n], ks.at[5 + n], kr.at[5 + n], dev) for n, (dev, p) in enumerate(
-        ((inner, 2 * h + 1 - lo), (outer, 2 * (1 - h) + 1 - lo), (diag, 2 * (1 - h) + lo)))]
-    shares = [remote(tq.at[to], blk.at[s, x], ks.at[8 + n], kr.at[8 + n], dev) for n, (dev, to) in enumerate(
-        ((inner, h), (outer, 1 - h), (diag, 1 - h)))]
-    tx_core = remote(blk.at[s], blk.at[s], ks.at[11], kr.at[11], core)
+    kx_outer = remote(kx_out.at[pl.ds(2 * (1 - h), 2)], kx_ro, ks.at[5], kr.at[5], outer)
+    kx_inner = remote(kx_half, kx_ri, ks.at[6], kr.at[6], inner)
+    tx_inner = remote(tq.at[lo], tq.at[lo], ks.at[7], kr.at[7], inner)
+    tx_outer = remote(turned, blk.at[s, pl.ds(2 * h, 2)], ks.at[8], kr.at[8], outer)
+    tx_core = remote(blk.at[s], blk.at[s], ks.at[9], kr.at[9], core)
+
+    def kept(w):
+        return kx[pl.ds(pl.multiple_of((1 - s) * hv + h * nv, nv), nv), pl.ds(pl.multiple_of(w * hv, hv), hv)]
 
     def cross_send():
         kx_core.start()
@@ -299,26 +302,33 @@
             k = kx[pl.ds(pl.multiple_of(s * hv + (p // 2) * nv, nv), nv), w] + kx_rc[tile(p // 2), w]
             kx_out[p] = k.astype(KSEND)
             kx[pl.ds(pl.multiple_of((1 - s) * hv + (p // 2) * nv, nv), nv), w] = k
-        for q in quarters:
-            q.start()
+        kx_outer.start()
+
+    def cross_turn():
+        kx_outer.wait()
+        kx_half[...] = (kept(1 - lo) + kx_ro[1 - lo].astype(F32)).astype(KSEND)
+        kx_inner.start()
 
     def cross_tiles():
-        for q in quarters:
-            q.wait()
-        m = kx_rq[0].astype(F32) + kx_rq[1].astype(F32) + kx_rq[2].astype(F32)
-        m = m + kx[pl.ds(pl.multiple_of((1 - s) * hv + h * nv, nv), nv), pl.ds(pl.multiple_of(lo * hv, hv), hv)]
+        kx_inner.wait()
+        m = kept(lo) + kx_ro[lo].astype(F32) + kx_ri[...].astype(F32)
         occ_k, occ_m = col, col + blocks
         for i in range(2):
-            t = amplitudes(m[:, i * nv:(i + 1) * nv], occ_m, 2 * s + h, occ_k, 2 * lo + i)
-            tq[0, i] = t.astype(BF16)
-            tq[1, i] = t.T.astype(BF16)
-        blk[s, x] = tq[h]
-        for q in shares:
-            q.start()
+            tq[lo, i] = amplitudes(m[:, i * nv:(i + 1) * nv], occ_m, 2 * s + h, occ_k, 2 * lo + i).astype(BF16)
+        tx_inner.start()
+
+    def cross_share():
+        tx_inner.wait()
+        for w in range(2):
+            for i in range(2):
+                t = tq[w, i]
+                back = t.astype(F32).T.astype(BF16)
+                blk[s, 2 * h + w, i] = jnp.where(h == 0, t, back)
+                turned[w, i] = jnp.where(h == 0, back, t)
+        tx_outer.start()
 
     def cross_swap():
-        for q in shares:
-            q.wait()
+        tx_outer.wait()
         tx_core.start()
 
     def cross_place():
@@ -339,8 +349,8 @@
                         tx[tile(2 * (xx % 2) + i), tile(2 * ss + xx // 2)] = blk[ss, xx, i]
 
     after = {}
-    for step, todo in zip(STEPS, (diag_send, diag_tiles, pack, unpack, land, diag_place, cross_send, cross_tiles,
-                                  cross_swap, cross_place), strict=True):
+    for step, todo in zip(STEPS, (diag_send, diag_tiles, pack, unpack, land, diag_place, cross_send, cross_turn,
+                                  cross_tiles, cross_share, cross_swap, cross_place), strict=True):
         after.setdefault(step, []).append(todo)
     begin = 0
     for step in sorted(after):
@@ -435,9 +445,12 @@
                 pltpu.VMEM((half_up, nv, nv), KSEND),
                 pltpu.VMEM((half_up, nv, nv), KSEND),
                 pltpu.VMEM((4, nv, flat // 2), KSEND),
-                pltpu.VMEM((3, nv, flat // 2), KSEND),
+                pltpu.VMEM((2, nv, flat // 2), KSEND),
+                pltpu.VMEM((nv, flat // 2), KSEND),
+                pltpu.VMEM((nv, flat // 2), KSEND),
                 pltpu.VMEM((flat, flat), BF16),
                 pltpu.VMEM((flat, flat), BF16),
+                pltpu.VMEM((2, 2, nv, nv), BF16),
                 pltpu.VMEM((2, 2, nv, nv), BF16),
                 pltpu.VMEM((2, 4, 2, nv, nv), BF16),
                 pltpu.VMEM((2, half_up, nv, nv), F32),

time: 137 us -> 144 us (1.051)
  Pallas kernels: 131 us -> 138 us
    pallas_call x1, Pallas kernels: 131 us -> 138 us  [run(): pl.pallas_call(functools.partial(kernel, dims, cap), out_shape=pltpu.VMEM...]
where the time goes in v5:
time: 144 us
  Pallas kernels  138 us (96%)
  local copies, waits for them, and re-layouts  2.74 us (2%)
    pallas_call x1, Pallas kernels, run(): pl.pallas_call(functools.partial(kernel, dims, cap), out_shape=pltpu.VMEM...  138 us

profile of v5, /device:TPU:1, one launch (start us, length us, event | category | flops | bytes accessed | tf_op | source)
XLA Modules:
  0.0 143.6 jit_solution(1985008657099401922)
XLA Ops:
  0.0 0.7 compare_convert_fusion.3
  0.7 0.1 reshape.46
  0.7 0.1 reduce_sum.9
  0.9 0.6 fusion.2
  2.2 138.8 %conditional.1 = (bf16[6000,4,128]{2,1,0:T(4,128)(2,1)S(1)}) conditional(s32[]{:T(128)} %clamp.3, (f32[128]{0:T(128)}, bf16[6000,4,128]{2,1,0:T(4,128)(2,1)}, f32[256]{0:T(256)}, s32[64]{0:T(128)}) %tuple.21, (f32[128]{0:T(128)}, bf16[6000,4,128]{2,1,0:T(4,128)(2,1)}, f32[256]{0:T(256)}, s32[64]{0:T(128)}) %tuple.21, ...), branch_computations={%region_2.0_spmd, %region_3.0_spmd, %region_4.0_spmd, %region_5.0_... | conditional | bytes 8 | solution.py:474
  2.4 138.2 %branch_2_fun.1 = bf16[24000,128]{1,0:T(8,128)(2,1)S(1)} custom-call(f32[256]{0:T(256)} %get-tuple-element.82.occ_energy, s32[64]{0:T(128)} %get-tuple-element.52.occ_count, f32[1,128]{1,0:T(1,128)} %bitcast.22, bf16[24000,128]{1,0:T(8,128)(2,1)} %bitcast.18), custom_call_target="tpu_custom_call" | custom-call | tf_op jit(solution)/shard_map/cond/branch_2_fun/pallas_call | solution.py:423
  140.9 2.7 %copy.26 = bf16[6000,4,128]{2,1,0:T(4,128)(2,1)} copy(bf16[6000,4,128]{2,1,0:T(4,128)(2,1)S(1)} %get-tuple-element.59) | data formatting | bytes 12288000
